TPU v7x, 256 devices: a whole 4x4x8 slice. The times are simulated.
256 devices in a mesh: row: 32 (over y_lo, z, core), col: 8 (over x, y_hi).
Axes of the slice: x: 4, y: 4 (y_hi: 2, y_lo: 2; y = y_hi * 2 + y_lo), z: 8, core: 2. Of those that a mesh axis runs over, the one named last changes fastest.
Arguments:
- pair_input: bfloat16 [512, 512, 128], P('row', 'col'), may hold values from -6 to 6
- norm_gain: float32 [128], replicated, may hold values from 0.1 to 1.9
- norm_bias: float32 [128], replicated, may hold values from -3 to 3
- weights: bfloat16 [4, 128, 128], replicated, may hold values from -0.5 to 0.5
- cotangent: bfloat16 [512, 512, 128], P('row', 'col'), may hold values from -0.29882812 to 0.29882812
Outputs:
- pair_grad: bfloat16 [512, 512, 128], P('row', 'col')
- weight_grad: float32 [4, 128, 128], replicated
- gain_grad: float32 [128], replicated
- bias_grad: float32 [128], replicated
All inputs are finite; a program needn't handle non-finite values.
Results may differ from a plain program's by a relative error of at most 0.0068.
Values may be sent and summed in bfloat16 or wider, within the bound.
A program may use at most 192 MiB of HBM per device.

v0:
```python
import jax
import jax.numpy as jnp
from jax import lax
from jax.sharding import PartitionSpec as P


def layer_norm(pair_tile, norm_gain, norm_bias, weights_flat):
    values = pair_tile.astype(jnp.float32)
    values = values.reshape(-1, values.shape[-1])
    average = jnp.mean(values, -1, keepdims=True)
    centred = values - average
    inverse = lax.rsqrt(jnp.mean(centred * centred, -1, keepdims=True) + 1e-05)
    scaled = centred * inverse
    normed = (scaled * norm_gain + norm_bias).astype(jnp.bfloat16)
    preact = jnp.dot(normed, weights_flat, preferred_element_type=jnp.float32)
    return (normed, scaled, inverse, preact)


def operands_of(preact, hidden, leading):
    sigmoid_first = jax.nn.sigmoid(preact[:, :hidden])
    sigmoid_second = jax.nn.sigmoid(preact[:, 2 * hidden : 3 * hidden])
    first = (sigmoid_first * preact[:, hidden : 2 * hidden]).astype(jnp.bfloat16)
    second = (sigmoid_second * preact[:, 3 * hidden :]).astype(jnp.bfloat16)
    return (first.reshape(leading + (hidden,)), second.reshape(leading + (hidden,)))


def local(pair_input, norm_gain, norm_bias, weights, cotangent):
    rows_here, cols_here, channels = pair_input.shape
    hidden = weights.shape[2]
    crop_size = rows_here * lax.axis_size("row")
    weights_flat = jnp.transpose(weights, (1, 0, 2)).reshape(channels, 4 * hidden)
    normed, scaled, inverse, preact = layer_norm(pair_input, norm_gain, norm_bias, weights_flat)
    first_tile, second_tile = operands_of(preact, hidden, (rows_here, cols_here))
    cotangent_rows = lax.all_gather(cotangent, "col", axis=1, tiled=True)
    cotangent_cols = lax.all_to_all(cotangent_rows, "row", split_axis=1, concat_axis=0, tiled=True)
    grad_first = jnp.einsum(
        "ijh,jkh->ikh",
        cotangent_rows,
        lax.all_gather(second_tile, "row", axis=0, tiled=True),
        preferred_element_type=jnp.float32,
    )
    grad_second = jnp.einsum(
        "ijh,ikh->jkh",
        cotangent_cols,
        lax.all_gather(first_tile, "row", axis=0, tiled=True),
        preferred_element_type=jnp.float32,
    )
    grad_first, grad_second = (grad_first, grad_second)
    grad_first = grad_first.reshape(-1, hidden)
    grad_second = grad_second.reshape(-1, hidden)
    sigmoid_first = jax.nn.sigmoid(preact[:, :hidden])
    sigmoid_second = jax.nn.sigmoid(preact[:, 2 * hidden : 3 * hidden])
    preact_grad = jnp.concatenate(
        [
            grad_first * preact[:, hidden : 2 * hidden] * sigmoid_first * (1.0 - sigmoid_first),
            grad_first * sigmoid_first,
            grad_second * preact[:, 3 * hidden :] * sigmoid_second * (1.0 - sigmoid_second),
            grad_second * sigmoid_second,
        ],
        1,
    ).astype(jnp.bfloat16)
    normed_grad = jnp.dot(preact_grad, weights_flat.T, preferred_element_type=jnp.float32)
    weight_part = jnp.dot(normed.T, preact_grad, preferred_element_type=jnp.float32)
    gain_part = jnp.sum(scaled * normed_grad, 0)
    bias_part = jnp.sum(normed_grad, 0)
    weight_sum, gain_sum, bias_sum = lax.psum((weight_part, gain_part, bias_part), ("row", "col"))
    factor = 1.0 / crop_size
    weight_grad = jnp.transpose(weight_sum.reshape(channels, 4, hidden), (1, 0, 2)) * factor
    gain_grad = gain_sum * factor
    bias_grad = bias_sum * factor
    scaled_grad = normed_grad * norm_gain
    pair_grad = inverse * (
        scaled_grad
        - jnp.mean(scaled_grad, -1, keepdims=True)
        - scaled * jnp.mean(scaled_grad * scaled, -1, keepdims=True)
    )
    pair_grad = pair_grad.reshape(rows_here, cols_here, channels).astype(jnp.bfloat16)
    return (pair_grad, weight_grad, gain_grad, bias_grad)


def solution(mesh):
    placed = (P("row", "col", None), P(), P(), P(), P("row", "col", None))
    return jax.shard_map(
        local,
        mesh=mesh,
        in_specs=placed,
        out_specs=(P("row", "col", None), P(), P(), P()),
        check_vma=False,
    )
```

profile of v0, /device:TPU:1, one launch (start us, length us, event | category | flops | bytes accessed | tf_op | source)
XLA Modules:
  0.0 632.2 jit_solution(418842024419603421)
XLA Ops:
  7.2 1.8 copy.40
  10.1 1.2 convert_reduce_fusion
  11.3 1.3 multiply_reduce_fusion.2
  12.7 1.3 add_convert_fusion.1
  14.7 1.2 copy.43
  16.0 1.2 copy.39
  17.2 56.5 %all-gather.6.cloned.1.call-done = bf16[16,512,128]{2,0,1:T(8,128)(2,1)} async-done(((bf16[16,64,128]{2,0,1:T(8,128)(2,1)}), bf16[16,512,128]{2,0,1:T(8,128)(2,1)}) %all-gather.6.cloned.1.call-update) | async-done | bytes 2097168 | tf_op jit(solution)/shard_map/all_gather | solution.py:34
  73.8 9.2 %all-to-all-start = ((bf16[16,512,128]{2,0,1:T(8,128)(2,1)}), bf16[16,512,128]{2,0,1:T(8,128)(2,1)}, u32[]{:S(2)}, u32[]{:S(2)}) async-start(bf16[16,512,128]{2,0,1:T(8,128)(2,1)} %all-gather.6.cloned.1.call-done), calls=%async_computation | async-start | bytes 4194304 | tf_op jit(solution)/shard_map/all_to_all | solution.py:35
  83.2 4.9 copy.41
  88.1 57.5 %all-to-all-done = bf16[16,512,128]{2,0,1:T(8,128)(2,1)} async-done(((bf16[16,512,128]{2,0,1:T(8,128)(2,1)}), bf16[16,512,128]{2,0,1:T(8,128)(2,1)}, u32[]{:S(2)}, u32[]{:S(2)}) %all-to-all-start) | async-done | bytes 2097184 | tf_op jit(solution)/shard_map/all_to_all | solution.py:35
  145.6 3.4 copy.45
  149.0 4.9 copy.46
  154.0 86.4 %all-gather.8.cloned.1.call-done = bf16[512,64,128]{1,0,2:T(8,128)(2,1)} async-done(((bf16[16,64,128]{1,0,2:T(8,128)(2,1)}), bf16[512,64,128]{1,0,2:T(8,128)(2,1)}) %all-gather.8.cloned.1.call-update) | async-done | bytes 8388624 | tf_op jit(solution)/shard_map/all_gather | solution.py:45
  240.4 8.7 %convolution_bitcast_fusion = f32[16,64,128]{1,0,2:T(8,128)S(1)} fusion(bf16[512,16,128]{0,1,2:T(8,128)(2,1)} %copy.46, bf16[512,64,128]{1,0,2:T(8,128)(2,1)} %all-gather.8.cloned.1.call-done), kind=kOutput, calls=%fused_computation | convolution fusion | flops 134217728 | bytes 11010048 | tf_op jit(solution)/shard_map/ijh,ikh->jkh/dot_general | solution.py:42
  249.1 1.3 copy.47
  250.3 113.8 %all-gather.4.cloned.1.call-done = bf16[512,64,128]{1,0,2:T(8,128)(2,1)} async-done(((bf16[16,64,128]{1,0,2:T(8,128)(2,1)}), bf16[512,64,128]{1,0,2:T(8,128)(2,1)}) %all-gather.4.cloned.1.call-update) | async-done | bytes 8388624 | tf_op jit(solution)/shard_map/all_gather | solution.py:39
  364.1 8.7 %convolution_bitcast_fusion.1 = f32[16,64,128]{1,0,2:T(8,128)S(1)} fusion(bf16[16,512,128]{1,0,2:T(8,128)(2,1)} %copy.41, bf16[512,64,128]{1,0,2:T(8,128)(2,1)} %all-gather.4.cloned.1.call-done), kind=kOutput, calls=%fused_computation.1 | convolution fusion | flops 134217728 | bytes 11010048 | tf_op jit(solution)/shard_map/ijh,jkh->ikh/dot_general | solution.py:36
  372.8 1.2 copy.42
  374.1 1.7 fusion.13
  376.5 1.1 fusion.15
  377.5 76.7 %all-reduce = (f32[128]{0:T(128)S(1)}, f32[128]{0:T(128)S(1)}) all-reduce(f32[128]{0:T(128)S(1)} %get-tuple-element.4, f32[128]{0:T(128)S(1)} %get-tuple-element.7), channel_id=1, replica_groups=mesh['row'=32,'col'=8] {'row','col'}, use_global_device_ids=true, to_apply=%region_6.0 | all-reduce | flops 256 | bytes 2048 | tf_op jit(solution)/shard_map/psum | solution.py:66
  454.3 1.3 multiply_convert_fusion
  456.1 167.9 %all-reduce.3.cloned.1.call-done = f32[128,512]{1,0:T(8,128)} async-done(((f32[128,512]{1,0:T(8,128)}), f32[128,512]{1,0:T(8,128)}) %all-reduce.3.cloned.1.call-update) | async-done | bytes 262160 | tf_op jit(solution)/shard_map/psum | solution.py:66
  624.0 1.7 bitcast_bitcast_fusion
  (24 shorter events, 3.3 us)
Async XLA Ops:
  7.2 66.6 %all-gather.6.cloned.1.call-start = ((), (), s32[]{:S(2)}) async-start(), calls=%async_computation.2 | async-start | bytes 2359296 | tf_op jit(solution)/shard_map/all_gather | solution.py:34
  9.1 231.3 %all-gather.8.cloned.1.call-start = ((), (), s32[]{:S(2)}) async-start(), calls=%async_computation.3 | async-start | bytes 17301504 | tf_op jit(solution)/shard_map/all_gather | solution.py:45
  15.9 348.2 %all-gather.4.cloned.1.call-start = ((), (), s32[]{:S(2)}) async-start(), calls=%async_computation.1 | async-start | bytes 17301504 | tf_op jit(solution)/shard_map/all_gather | solution.py:39
  73.8 71.8 %all-to-all-start = ((bf16[16,512,128]{2,0,1:T(8,128)(2,1)}), bf16[16,512,128]{2,0,1:T(8,128)(2,1)}, u32[]{:S(2)}, u32[]{:S(2)}) async-start(bf16[16,512,128]{2,0,1:T(8,128)(2,1)} %all-gather.6.cloned.1.call-done), calls=%async_computation | async-start | bytes 4194304 | tf_op jit(solution)/shard_map/all_to_all | solution.py:35
  83.0 541.0 %all-reduce.3.cloned.1.call-start = ((), (), s32[]{:S(2)}) async-start(), calls=%async_computation.4 | async-start | bytes 524288 | tf_op jit(solution)/shard_map/psum | solution.py:66
  374.1 1.7 copy-start
  374.1 1.7 copy-start.1
  374.1 1.7 copy-start.2
Sparse Core Ops, SparseCore 0:
  11.2 62.5 all-gather.5
  75.5 164.7 all-gather.7
  242.1 121.9 all-gather.3
  377.7 246.3 all-reduce.2
where the time goes:
time: 633 us; the launch traced here: 632 us
  waiting for transfers between devices  482 us (76%)
  blocking collectives  76.7 us (12%)
  local copies, waits for them, and re-layouts  21.2 us (3%)
  matrix products  19.5 us (3%)
  between operations  13.9 us (2%)
  starting transfers between devices  9.39 us (1%)
  other arithmetic  9.3 us (1%)
    psum x1, waiting for transfers between devices, local(): lax.psum((weight_part, gain_part, bias_part), ('row', 'col'))  168 us
    all_gather x1, waiting for transfers between devices, local(): lax.all_gather(second_tile, 'row', axis=0, tiled=True)  114 us
    all_gather x1, waiting for transfers between devices, local(): lax.all_gather(first_tile, 'row', axis=0, tiled=True)  86.4 us
    psum x1, blocking collectives, local(): lax.psum((weight_part, gain_part, bias_part), ('row', 'col'))  76.7 us
    all_to_all x1, waiting for transfers between devices, local(): lax.all_to_all(cotangent_rows, 'row', split_axis=1, concat_axis=0, tiled=...  57.5 us
    all_gather x1, waiting for transfers between devices, local(): cotangent_rows = lax.all_gather(cotangent, 'col', axis=1, tiled=True)  56.5 us
  transfers between devices with their start and end apart: 5, of which 5 were waited for; matrix products, arithmetic and copies ran while one was open for 5% of the time, Pallas kernels for 0%

commit v1 on v0

v1 whole, which is shorter than its diff:
```python
import jax
import jax.numpy as jnp
from jax import lax
from jax.experimental import pallas as pl
from jax.experimental.pallas import tpu as pltpu
from jax.sharding import PartitionSpec as P

MESH = pl.DeviceIdType.MESH
F32 = jnp.float32
BF16 = jnp.bfloat16

ROWS, COLS, DEPTH, XS = 32, 8, 8, 4
R, W, H, N = 16, 64, 128, 512
PAIRS = R * W
OWN = H // ROWS // 2
PLANES = H // 2

COT, OPS, SECOND, FIRST, PART, DEEP, WHOLE, SMALL_Z, SMALL_COL, SMALL_ROW, RING = range(11)


def nt(a, b):
    return lax.dot_general(a, b, (((1,), (1,)), ((), ())), preferred_element_type=F32)


def tn(a, b):
    return lax.dot_general(a, b, (((0,), (0,)), ((), ())), preferred_element_type=F32)


def kernel(
    pair_ref, gain_ref, bias_ref, w_ref, cot_ref,
    out_ref, wg_ref, gg_ref, bg_ref,
    stage, send_cot, send_ops, cots, ops, blocks, acc, out_first, out_second, got_first, got_second,
    factors, scaled, normed, inverse, w_t, w_cat, grads, w_part, parts, deeps, wholes, small_z, small_col, small_row,
    send_sem, recv_sem, ring_sem, local_sem,
):
    row, col = lax.axis_index("row"), lax.axis_index("col")
    z, core, y_lo = lax.rem(row // 2, DEPTH), lax.rem(row, 2), row // (2 * DEPTH)
    x, y_hi = col // 2, lax.rem(col, 2)
    left_lanes = lax.broadcasted_iota(jnp.int32, (W, 2 * W), 1) < W
    eye = (
        lax.broadcasted_iota(jnp.int32, (H, H), 0) == lax.broadcasted_iota(jnp.int32, (H, H), 1)
    ).astype(F32).astype(BF16)

    def plane_row(s):
        return (s // 2) * (2 * DEPTH) + z * 2 + lax.rem(s, 2)

    def send(src, dst, kind, device, arrived=None):
        pltpu.make_async_remote_copy(
            src_ref=src,
            dst_ref=dst,
            send_sem=send_sem.at[kind],
            recv_sem=recv_sem.at[kind] if arrived is None else arrived,
            device_id=device,
            device_id_type=MESH,
        ).start()

    def wait(ref, sem):
        pltpu.make_async_copy(ref, ref, sem).wait()

    def rows_of(p):
        return pl.ds(pl.multiple_of(p * R, R), R)

    def planes_of(p):
        return pl.ds(p * OWN, OWN)

    def spread(t, value):
        low, high = value[:PLANES], value[PLANES:]
        stage[pl.ds(2 * t * PLANES, PLANES), :] = jnp.where(left_lanes, low, pltpu.roll(high, W, 1))
        stage[pl.ds((2 * t + 1) * PLANES, PLANES), :] = jnp.where(left_lanes, pltpu.roll(low, W, 1), high)

    barrier = pltpu.get_barrier_semaphore()

    @pl.loop(1, ROWS)
    def _(d):
        pl.semaphore_signal(barrier, inc=1, device_id=(lax.rem(row + d, ROWS), col), device_id_type=MESH)

    @pl.loop(0, 4 * (COLS - 1))
    def _(d):
        pl.semaphore_signal(
            barrier,
            inc=1,
            device_id=(plane_row(d // (COLS - 1)), lax.rem(col + 1 + lax.rem(d, COLS - 1), COLS)),
            device_id_type=MESH,
        )

    for t in range(R // 2):
        spread(t, nt(eye, cot_ref[t * 2 * W : (t + 1) * 2 * W, :]))

    @pl.loop(0, PLANES, unroll=8)
    def _(h):
        send_cot[h] = stage[pl.ds(h, R, stride=PLANES), :].astype(BF16)

    pl.semaphore_wait(barrier, ROWS - 1 + 4 * (COLS - 1))

    @pl.loop(1, ROWS)
    def _(d):
        p = lax.rem(row + d, ROWS)
        send(send_cot.at[planes_of(p)], cots.at[col, :, rows_of(row), :], COT, (p, col))

    own_cot = pltpu.make_async_copy(send_cot.at[planes_of(row)], cots.at[col, :, rows_of(row), :], local_sem.at[COT])
    own_cot.start()

    gain = jnp.transpose(jnp.broadcast_to(gain_ref[...], (H, H)))
    bias = jnp.transpose(jnp.broadcast_to(bias_ref[...], (H, H)))
    for m in range(4):
        w_t[m * H : (m + 1) * H, :] = jnp.transpose(w_ref[m].astype(F32)).astype(BF16)
        w_cat[:, m * H : (m + 1) * H] = w_ref[m]
    for t in range(R // 2):
        lanes = slice(t * 2 * W, (t + 1) * 2 * W)
        values = nt(eye, pair_ref[lanes, :])
        centred = values - jnp.mean(values, 0, keepdims=True)
        inv = lax.rsqrt(jnp.mean(centred * centred, 0, keepdims=True) + 1e-05)
        scale = centred * inv
        inverse[t : t + 1, :] = inv
        scaled[:, lanes] = scale
        normed[:, lanes] = (scale * gain + bias).astype(BF16)
    for side in range(2):
        for t in range(R // 2):
            lanes = slice(t * 2 * W, (t + 1) * 2 * W)
            pre = jnp.dot(w_t[2 * side * H : 2 * (side + 1) * H, :], normed[:, lanes], preferred_element_type=F32)
            gate, value = jax.nn.sigmoid(pre[:H]), pre[H:]
            product = gate * value
            factors[2 * side * H : (2 * side + 1) * H, lanes] = product * (1.0 - gate)
            factors[(2 * side + 1) * H : 2 * (side + 1) * H, lanes] = gate
            spread(t, product)

        @pl.loop(0, ROWS, unroll=4)
        def _(p):
            for k in range(OWN):
                send_ops[p, side * OWN + k] = stage[pl.ds(p * OWN + k, R, stride=PLANES), :].astype(BF16)

    @pl.loop(1, ROWS)
    def _(d):
        p = lax.rem(row + d, ROWS)
        send(send_ops.at[p], ops.at[:, rows_of(row), :], OPS, (p, col))

    own_ops = pltpu.make_async_copy(send_ops.at[row], ops.at[:, rows_of(row), :], local_sem.at[OPS])
    own_ops.start()

    own_cot.wait()
    wait(cots.at[0, :, : N - R, :], recv_sem.at[COT])
    mate = col + 1 - 2 * y_hi
    right_x, left_x, far_x = lax.rem(x + 1, XS), lax.rem(x + XS - 1, XS), lax.rem(x + 2, XS)
    right, left = right_x * 2 + y_hi, left_x * 2 + y_hi

    def pass_on(q, k, to):
        send(cots.at[q, k], cots.at[q, k], RING, (row, to), ring_sem.at[q, k])

    def arrived(q, k):
        wait(cots.at[q, k], ring_sem.at[q, k])

    pass_on(col, 0, right)
    pass_on(col, 1, left)
    pass_on(col, 0, mate)
    pass_on(col, 1, mate)
    pass_on(col, 1, right)
    pass_on(col, 0, left)
    arrived(mate, 0)
    pass_on(mate, 0, right)
    pass_on(mate, 0, left)
    arrived(mate, 1)
    pass_on(mate, 1, left)
    pass_on(mate, 1, right)
    arrived(left, 0)
    pass_on(left, 0, right)
    arrived(right, 1)
    pass_on(right, 1, left)

    own_ops.wait()
    wait(ops.at[:, : N - R, :], recv_sem.at[OPS])
    for k in range(OWN):
        for q in range(COLS):
            block = ops[OWN + k, q * W : (q + 1) * W, :].astype(F32)
            blocks[k, q * 2 * W : q * 2 * W + W, :] = jnp.where(left_lanes, block, 0.0).astype(BF16)
            blocks[k, q * 2 * W + W : (q + 1) * 2 * W, :] = jnp.where(left_lanes, 0.0, block).astype(BF16)

    def products(at, opening):
        for k in range(OWN):
            cot = jnp.concatenate([cots[2 * at, k], cots[2 * at + 1, k]], 1)
            term = jnp.dot(
                cot, blocks[k, pl.ds(pl.multiple_of(at * 4 * W, 4 * W), 4 * W), :], preferred_element_type=F32
            )
            if opening:
                acc[k] = term
            else:
                acc[k] += term
            both = tn(cot, ops[k])
            for y in range(2):
                out_second[k, pl.ds(pl.multiple_of((2 * at + y) * W, W), W), :] = jnp.where(
                    left_lanes, both[2 * y * W : (2 * y + 1) * W], both[(2 * y + 1) * W : 2 * (y + 1) * W]
                ).astype(BF16)

        @pl.loop(0, ROWS // XS)
        def _(d):
            p = at * (ROWS // XS) + d

            @pl.when(p != row)
            def _():
                send(out_second.at[:, rows_of(p), :], got_second.at[planes_of(row)], SECOND, (p, col))

            @pl.when(p == row)
            def _():
                copy = pltpu.make_async_copy(
                    out_second.at[:, rows_of(p), :], got_second.at[planes_of(row)], local_sem.at[SECOND]
                )
                copy.start()
                copy.wait()

    products(x, True)
    mate_left, mate_right = left_x * 2 + 1 - y_hi, right_x * 2 + 1 - y_hi
    arrived(mate_left, 0)
    pass_on(mate_left, 0, right)
    arrived(mate_right, 1)
    pass_on(mate_right, 1, left)
    arrived(left, 1)
    arrived(mate_left, 1)
    products(left_x, False)
    arrived(right, 0)
    arrived(mate_right, 0)
    products(right_x, False)
    for k in range(2):
        arrived(far_x * 2, k)
        arrived(far_x * 2 + 1, k)
    products(far_x, False)

    for k in range(OWN):
        out_first[k] = acc[k].astype(BF16)

    @pl.loop(1, ROWS)
    def _(d):
        p = lax.rem(row + d, ROWS)
        send(out_first.at[:, rows_of(p), :], got_first.at[planes_of(row)], FIRST, (p, col))

    own_first = pltpu.make_async_copy(
        out_first.at[:, rows_of(row), :], got_first.at[planes_of(row)], local_sem.at[FIRST]
    )
    own_first.start()

    def gather_in(side, got):
        @pl.loop(0, PLANES, unroll=8)
        def _(h):
            stage[pl.ds(pl.multiple_of(h * R, R), R), :] = got[h].astype(F32)

        for t in range(R // 2):
            lanes = slice(t * 2 * W, (t + 1) * 2 * W)
            even = stage[pl.ds(2 * t, PLANES, stride=R), :]
            odd = stage[pl.ds(2 * t + 1, PLANES, stride=R), :]
            grad = jnp.concatenate(
                [
                    jnp.where(left_lanes, even, pltpu.roll(odd, W, 1)),
                    jnp.where(left_lanes, pltpu.roll(even, W, 1), odd),
                ],
                0,
            )
            for m in (2 * side, 2 * side + 1):
                grads[m * H : (m + 1) * H, lanes] = (grad * factors[m * H : (m + 1) * H, lanes]).astype(BF16)

    def weight_part(side):
        part = nt(normed[...], grads[2 * side * H : 2 * (side + 1) * H, :])
        for m in range(2):
            w_part[(2 * side + m) * H : (2 * side + m + 1) * H, :] = part[:, m * H : (m + 1) * H]

    wait(got_second.at[: PLANES - OWN], recv_sem.at[SECOND])
    gather_in(1, got_second)
    weight_part(1)
    own_first.wait()
    wait(got_first.at[: PLANES - OWN], recv_sem.at[FIRST])
    gather_in(0, got_first)
    weight_part(0)

    spot = (y_lo * 2 + core) * COLS + col

    def of_plane(d):
        g = lax.rem(spot + d, 4 * COLS)
        return g, (plane_row(g // COLS), lax.rem(g, COLS))

    @pl.loop(1, 4 * COLS)
    def _(d):
        g, device = of_plane(d)
        send(w_part.at[rows_of(g), :], parts.at[spot], PART, device)

    parts[spot] = w_part[rows_of(spot), :]

    gain_sum = jnp.zeros((H, 2 * W), F32)
    bias_sum = jnp.zeros((H, 2 * W), F32)
    for t in range(R // 2):
        lanes = slice(t * 2 * W, (t + 1) * 2 * W)
        grad = jnp.dot(w_cat[...], grads[:, lanes], preferred_element_type=F32)
        scale = scaled[:, lanes]
        gain_sum += grad * scale
        bias_sum += grad
        grad = grad * gain
        pair = inverse[t : t + 1, :] * (
            grad - jnp.mean(grad, 0, keepdims=True) - scale * jnp.mean(grad * scale, 0, keepdims=True)
        )
        out_ref[lanes, :] = jnp.transpose(pair).astype(BF16)
    gain_sum = jnp.sum(jnp.transpose(gain_sum), 0, keepdims=True)
    bias_sum = jnp.sum(jnp.transpose(bias_sum), 0, keepdims=True)
    small_z[z] = jnp.concatenate([gain_sum, bias_sum, jnp.zeros((6, H), F32)], 0)

    def z_peer(d):
        return (y_lo * 2 * DEPTH + lax.rem(z + d, DEPTH) * 2 + core, col)

    @pl.loop(1, DEPTH)
    def _(d):
        send(small_z.at[z], small_z.at[z], SMALL_Z, z_peer(d))

    wait(parts.at[: 4 * COLS - 1], recv_sem.at[PART])
    deeps[z] = jnp.sum(parts[...], 0)

    @pl.loop(1, DEPTH)
    def _(d):
        send(deeps.at[z], deeps.at[z], DEEP, z_peer(d))

    wait(small_z.at[: DEPTH - 1], recv_sem.at[SMALL_Z])
    small_col[col] = jnp.sum(small_z[...], 0)

    @pl.loop(1, COLS)
    def _(d):
        send(small_col.at[col], small_col.at[col], SMALL_COL, (row, lax.rem(col + d, COLS)))

    wait(deeps.at[: DEPTH - 1], recv_sem.at[DEEP])
    wholes[spot] = jnp.sum(deeps[...], 0) * (1.0 / N)

    @pl.loop(1, 4 * COLS)
    def _(d):
        _, device = of_plane(d)
        send(wholes.at[spot], wholes.at[spot], WHOLE, device)

    wait(small_col.at[: COLS - 1], recv_sem.at[SMALL_COL])
    quarter = y_lo * 2 + core
    small_row[quarter] = jnp.sum(small_col[...], 0)

    @pl.loop(1, 4)
    def _(d):
        send(small_row.at[quarter], small_row.at[quarter], SMALL_ROW, (plane_row(lax.rem(quarter + d, 4)), col))

    wait(small_row.at[:3], recv_sem.at[SMALL_ROW])
    total = jnp.sum(small_row[...], 0) * (1.0 / N)
    gg_ref[...] = total[0:1]
    bg_ref[...] = total[1:2]

    wait(wholes.at[: 4 * COLS - 1], recv_sem.at[WHOLE])
    wg_ref[...] = wholes[...].reshape(4 * H, H)

    wait(cots.at[0, :, : N - R, :], send_sem.at[COT])
    wait(ops.at[:, : N - R, :], send_sem.at[OPS])
    wait(cots.at[: COLS - 1], send_sem.at[RING])
    wait(got_second.at[: PLANES - OWN], send_sem.at[SECOND])
    wait(got_first.at[: PLANES - OWN], send_sem.at[FIRST])
    wait(parts.at[: 4 * COLS - 1], send_sem.at[PART])
    wait(deeps.at[: DEPTH - 1], send_sem.at[DEEP])
    wait(wholes.at[: 4 * COLS - 1], send_sem.at[WHOLE])
    wait(small_z.at[: DEPTH - 1], send_sem.at[SMALL_Z])
    wait(small_col.at[: COLS - 1], send_sem.at[SMALL_COL])
    wait(small_row.at[:3], send_sem.at[SMALL_ROW])


def local(pair_input, norm_gain, norm_bias, weights, cotangent):
    vmem = pl.BlockSpec(memory_space=pltpu.VMEM)
    out, weight_grad, gain_grad, bias_grad = pl.pallas_call(
        kernel,
        out_shape=(
            jax.ShapeDtypeStruct((PAIRS, H), BF16),
            jax.ShapeDtypeStruct((4 * H, H), F32),
            jax.ShapeDtypeStruct((1, H), F32),
            jax.ShapeDtypeStruct((1, H), F32),
        ),
        in_specs=[vmem] * 5,
        out_specs=(vmem,) * 4,
        scratch_shapes=[
            pltpu.VMEM((PAIRS, 2 * W), F32),
            pltpu.VMEM((PLANES, R, 2 * W), BF16),
            pltpu.VMEM((ROWS, 2 * OWN, R, 2 * W), BF16),
            pltpu.VMEM((COLS, OWN, N, 2 * W), BF16),
            pltpu.VMEM((2 * OWN, N, 2 * W), BF16),
            pltpu.VMEM((OWN, 2 * N, 2 * W), BF16),
            pltpu.VMEM((OWN, N, 2 * W), F32),
            pltpu.VMEM((OWN, N, 2 * W), BF16),
            pltpu.VMEM((OWN, N, 2 * W), BF16),
            pltpu.VMEM((PLANES, R, 2 * W), BF16),
            pltpu.VMEM((PLANES, R, 2 * W), BF16),
            pltpu.VMEM((4 * H, PAIRS), F32),
            pltpu.VMEM((H, PAIRS), F32),
            pltpu.VMEM((H, PAIRS), BF16),
            pltpu.VMEM((R // 2, 2 * W), F32),
            pltpu.VMEM((4 * H, H), BF16),
            pltpu.VMEM((H, 4 * H), BF16),
            pltpu.VMEM((4 * H, PAIRS), BF16),
            pltpu.VMEM((4 * H, H), F32),
            pltpu.VMEM((4 * COLS, R, H), F32),
            pltpu.VMEM((DEPTH, R, H), F32),
            pltpu.VMEM((4 * COLS, R, H), F32),
            pltpu.VMEM((DEPTH, 8, H), F32),
            pltpu.VMEM((COLS, 8, H), F32),
            pltpu.VMEM((4, 8, H), F32),
            pltpu.SemaphoreType.DMA((11,)),
            pltpu.SemaphoreType.DMA((11,)),
            pltpu.SemaphoreType.DMA((COLS, OWN)),
            pltpu.SemaphoreType.DMA((4,)),
        ],
        compiler_params=pltpu.CompilerParams(
            collective_id=0, has_side_effects=True, vmem_limit_bytes=40 * 1024 * 1024
        ),
        name="triangle_backward",
    )(
        pair_input.reshape(PAIRS, H),
        norm_gain.reshape(1, H),
        norm_bias.reshape(1, H),
        weights,
        cotangent.reshape(PAIRS, H),
    )
    return (
        out.reshape(R, W, H),
        weight_grad.reshape(4, H, H),
        gain_grad.reshape(H),
        bias_grad.reshape(H),
    )


def solution(mesh):
    placed = (P("row", "col", None), P(), P(), P(), P("row", "col", None))
    return jax.shard_map(
        local,
        mesh=mesh,
        in_specs=placed,
        out_specs=(P("row", "col", None), P(), P(), P()),
        check_vma=False,
    )
```

time: 633 us -> 80 us (0.13)
  waiting for transfers between devices: 482 us -> 0 us
  blocking collectives: 76.7 us -> 0 us
  Pallas kernels: 0 us -> 73.2 us
  matrix products: 19.5 us -> 0 us
  local copies, waits for them, and re-layouts: 21.2 us -> 5.89 us
  between operations: 13.9 us -> 0.66 us
  starting transfers between devices: 9.39 us -> 0 us
  other arithmetic: 9.3 us -> 0 us
    all_gather x3 -> x0, waiting for transfers between devices: 257 us -> none  [the longest x1 114 us: local(): lax.all_gather(second_tile, 'row', axis=0, tiled=True)]
    psum x1 -> x0, waiting for transfers between devices: 168 us -> none  [local(): lax.psum((weight_part, gain_part, bias_part), ('row', 'col'))]
    psum x1 -> x0, blocking collectives: 76.7 us -> none  [local(): lax.psum((weight_part, gain_part, bias_part), ('row', 'col'))]
    pallas_call x0 -> x1, Pallas kernels: none -> 73.2 us  [local(): pl.pallas_call(kernel, out_shape=(jax.ShapeDtypeStruct((PAIRS, H), BF16),...]
    all_to_all x1 -> x0, waiting for transfers between devices: 57.5 us -> none  [local(): lax.all_to_all(cotangent_rows, 'row', split_axis=1, concat_axis=0, tiled=...]
    dot_general x5 -> x0, matrix products: 19.5 us -> none  [the longest x1 8.7 us: local(): jnp.einsum('ijh,ikh->jkh', cotangent_cols, lax.all_gather(first_tile, 'ro...]
    all_to_all x1 -> x0, starting transfers between devices: 9.23 us -> none  [local(): lax.all_to_all(cotangent_rows, 'row', split_axis=1, concat_axis=0, tiled=...]
    all_to_all x2 -> x0, local copies, waits for them, and re-layouts: 8.37 us -> none  [local(): lax.all_to_all(cotangent_rows, 'row', split_axis=1, concat_axis=0, tiled=...]
  transfers between devices with their start and end apart: 5 -> 0, of which waited for: 5 -> 0; matrix products, arithmetic and copies ran while one was open for 5% -> 0% of each run, Pallas kernels for 0% -> 0%
where the time goes in v1:
time: 80 us; the launch traced here: 79.8 us
  Pallas kernels  73.2 us (92%)
  local copies, waits for them, and re-layouts  5.89 us (7%)
    pallas_call x1, Pallas kernels, local(): pl.pallas_call(kernel, out_shape=(jax.ShapeDtypeStruct((PAIRS, H), BF16),...  73.2 us
    unnamed x14, local copies, waits for them, and re-layouts  5.89 us

profile of v1, /device:TPU:1, one launch (start us, length us, event | category | flops | bytes accessed | tf_op | source)
XLA Modules:
  0.0 79.8 jit_solution(2718209909552356632)
XLA Ops:
  0.6 0.0 copy-start.3
  0.6 0.0 copy-start.4
  0.7 0.6 copy-done.3
  1.3 0.0 copy-done.4
  1.3 0.0 copy-start
  1.3 0.9 %copy-done = bf16[16,64,128]{2,1,0:T(8,128)(2,1)S(1)} copy-done((bf16[16,64,128]{2,1,0:T(8,128)(2,1)S(1)}, bf16[16,64,128]{2,1,0:T(8,128)(2,1)}, u32[]{:S(2)}) %copy-start) | copy-done | bytes 262168
  2.3 0.0 copy-start.1
  2.3 0.9 %copy-done.1 = bf16[16,64,128]{2,1,0:T(8,128)(2,1)S(1)} copy-done((bf16[16,64,128]{2,1,0:T(8,128)(2,1)S(1)}, bf16[16,64,128]{2,1,0:T(8,128)(2,1)}, u32[]{:S(2)}) %copy-start.1) | copy-done | bytes 262168
  3.2 0.0 copy-start.2
  3.2 0.9 %copy-done.2 = bf16[4,128,128]{2,1,0:T(8,128)(2,1)S(1)} copy-done((bf16[4,128,128]{2,1,0:T(8,128)(2,1)S(1)}, bf16[4,128,128]{2,1,0:T(8,128)(2,1)}, u32[]{:S(2)}) %copy-start.2) | copy-done | bytes 131096
  4.1 73.2 %triangle_backward.1 = (bf16[1024,128]{1,0:T(8,128)(2,1)S(1)}, f32[512,128]{1,0:T(8,128)S(1)}, f32[1,128]{1,0:T(1,128)S(1)}, f32[1,128]{1,0:T(1,128)S(1)}) custom-call(bf16[1024,128]{1,0:T(8,128)(2,1)S(1)} %bitcast.8, f32[1,128]{1,0:T(1,128)S(1)} %bitcast.12, f32[1,128]{1,0:T(1,128)S(1)} %bitcast.13, bf16[4,128,128]{2,1,0:T(8,128)(2,1)S(1)} %copy-done.2, ...), custom_call_target="tpu_custom_call" | custom-call | tf_op jit(solution)/shard_map/triangle_backward/pallas_call | solution.py:361
  77.4 0.7 copy.13
  78.1 0.7 copy.14
  78.8 0.5 copy.15
  79.3 0.5 copy.16
Async XLA Ops:
  0.6 0.7 copy-start.3
  0.6 0.7 copy-start.4
  1.3 0.9 %copy-start = (bf16[16,64,128]{2,1,0:T(8,128)(2,1)S(1)}, bf16[16,64,128]{2,1,0:T(8,128)(2,1)}, u32[]{:S(2)}) copy-start(bf16[16,64,128]{2,1,0:T(8,128)(2,1)} %param.5) | copy-start | bytes 786436
  2.3 0.9 %copy-start.1 = (bf16[16,64,128]{2,1,0:T(8,128)(2,1)S(1)}, bf16[16,64,128]{2,1,0:T(8,128)(2,1)}, u32[]{:S(2)}) copy-start(bf16[16,64,128]{2,1,0:T(8,128)(2,1)} %param.9) | copy-start | bytes 786436
  3.2 0.9 %copy-start.2 = (bf16[4,128,128]{2,1,0:T(8,128)(2,1)S(1)}, bf16[4,128,128]{2,1,0:T(8,128)(2,1)}, u32[]{:S(2)}) copy-start(bf16[4,128,128]{2,1,0:T(8,128)(2,1)} %w_ref.1) | copy-start | bytes 393220

commit v2 on v1

v2 whole, which is shorter than its diff:
```python
import jax
import jax.numpy as jnp
from jax import lax
from jax.experimental import pallas as pl
from jax.experimental.pallas import tpu as pltpu
from jax.sharding import PartitionSpec as P

MESH = pl.DeviceIdType.MESH
F32 = jnp.float32
BF16 = jnp.bfloat16

ROWS, COLS, DEPTH, XS, YS = 32, 8, 8, 4, 2
R, W, H, N = 16, 64, 128, 512
PAIRS = R * W
BAND = ROWS * YS
SPOTS = COLS * 4
PART = 4 * H // SPOTS // 2

COT, OP_FIRST, OP_SECOND, FIRST, SECOND, PART_FIRST, PART_SECOND, DEEP, WHOLE, SMALL_Z, SMALL_COL, SMALL_ROW, RING = range(13)


def nt(a, b):
    return lax.dot_general(a, b, (((1,), (1,)), ((), ())), preferred_element_type=F32)


def tn(a, b):
    return lax.dot_general(a, b, (((0,), (0,)), ((), ())), preferred_element_type=F32)


def kernel(
    pair_hbm, gain_hbm, bias_hbm, w_hbm, cot_hbm,
    out_ref, wg_ref, gg_ref, bg_ref,
    pair_ref, gain_ref, bias_ref, w_ref, cot_ref,
    stage, send_cot, send_first, send_second, cots, firsts, seconds, blocks, out_first, out_second, got_first, got_second,
    factors, scaled, normed, inverse, w_t, w_cat, grads, normed_grad, w_part, parts, deeps, wholes, small_z, small_col, small_row,
    send_sem, recv_sem, ring_sem, local_sem, load_sem,
):
    row, col = lax.axis_index("row"), lax.axis_index("col")
    z, core, y_lo = lax.rem(row // 2, DEPTH), lax.rem(row, 2), row // (2 * DEPTH)
    x, y_hi = col // YS, lax.rem(col, YS)
    y = y_hi * 2 + y_lo
    plane = y_hi * ROWS + row

    loads = [
        pltpu.make_async_copy(src, dst, load_sem.at[i])
        for i, (src, dst) in enumerate(
            ((cot_hbm, cot_ref), (pair_hbm, pair_ref), (w_hbm, w_ref), (gain_hbm, gain_ref), (bias_hbm, bias_ref))
        )
    ]
    for load in loads:
        load.start()

    left_lanes = lax.broadcasted_iota(jnp.int32, (W, 2 * W), 1) < W
    eye = (
        lax.broadcasted_iota(jnp.int32, (H, H), 0) == lax.broadcasted_iota(jnp.int32, (H, H), 1)
    ).astype(F32).astype(BF16)

    def plane_row(s):
        return (s // 2) * (2 * DEPTH) + z * 2 + lax.rem(s, 2)

    def send(src, dst, kind, device, arrived=None):
        pltpu.make_async_remote_copy(
            src_ref=src,
            dst_ref=dst,
            send_sem=send_sem.at[kind],
            recv_sem=recv_sem.at[kind] if arrived is None else arrived,
            device_id=device,
            device_id_type=MESH,
        ).start()

    def wait(ref, sem):
        pltpu.make_async_copy(ref, ref, sem).wait()

    def rows_of(p):
        return pl.ds(pl.multiple_of(p * R, R), R)

    near = []
    for dy in (2, 1, 3, 0):
        other_y = lax.rem(y + dy, 4)
        for dc in (1, 0):
            near.append((other_y // 2, lax.rem(other_y, 2) * (2 * DEPTH) + lax.rem(core + dc, 2)))

    def each_of_band(act):
        @pl.loop(0, DEPTH - 1)
        def _(s):
            dz = DEPTH // 2 + ((s + 1) // 2) * (1 - 2 * lax.rem(s, 2))
            base = lax.rem(z + dz, DEPTH) * 2
            for there, offset in near:
                act(there, base + offset)

        for there, offset in near[:-1]:
            act(there, z * 2 + offset)

    barrier = pltpu.get_barrier_semaphore()
    right_x, left_x, far_x = lax.rem(x + 1, XS), lax.rem(x + XS - 1, XS), lax.rem(x + 2, XS)
    right, left = right_x * YS + y_hi, left_x * YS + y_hi

    def greet(there, p):
        pl.semaphore_signal(barrier, inc=1, device_id=(p, x * YS + there), device_id_type=MESH)

    each_of_band(greet)
    for to in (right, left):
        pl.semaphore_signal(barrier, inc=1, device_id=(row, to), device_id_type=MESH)

    def spread(t, value):
        low, high = value[:BAND], value[BAND:]
        stage[pl.ds(2 * t * BAND, BAND), :] = jnp.where(left_lanes, low, pltpu.roll(high, W, 1))
        stage[pl.ds((2 * t + 1) * BAND, BAND), :] = jnp.where(left_lanes, pltpu.roll(low, W, 1), high)

    def to_planes(planes):
        @pl.loop(0, BAND, unroll=8)
        def _(h):
            planes[h] = stage[pl.ds(h, R, stride=BAND), :].astype(BF16)

    def scatter(planes, dst, kind):
        def act(there, p):
            send(planes.at[there * ROWS + p], dst, kind, (p, x * YS + there))

        each_of_band(act)
        own = pltpu.make_async_copy(planes.at[plane], dst, local_sem.at[kind])
        own.start()
        return own

    loads[0].wait()
    for t in range(R // 2):
        spread(t, nt(eye, cot_ref[t * 2 * W : (t + 1) * 2 * W, :]))
    to_planes(send_cot)
    pl.semaphore_wait(barrier, BAND - 1 + 2)
    own_cot = scatter(send_cot, cots.at[x, y_hi, rows_of(row), :], COT)

    for load in loads[1:]:
        load.wait()
    gain = jnp.transpose(jnp.broadcast_to(gain_ref[...], (H, H)))
    bias = jnp.transpose(jnp.broadcast_to(bias_ref[...], (H, H)))
    for m in range(4):
        w_t[m * H : (m + 1) * H, :] = jnp.transpose(w_ref[m].astype(F32)).astype(BF16)
        w_cat[:, m * H : (m + 1) * H] = w_ref[m]
    for t in range(R // 2):
        lanes = slice(t * 2 * W, (t + 1) * 2 * W)
        values = nt(eye, pair_ref[lanes, :])
        centred = values - jnp.mean(values, 0, keepdims=True)
        inv = lax.rsqrt(jnp.mean(centred * centred, 0, keepdims=True) + 1e-05)
        scale = centred * inv
        inverse[t : t + 1, :] = inv
        scaled[:, lanes] = scale
        normed[:, lanes] = (scale * gain + bias).astype(BF16)

    def gated(side, planes):
        for t in range(R // 2):
            lanes = slice(t * 2 * W, (t + 1) * 2 * W)
            pre = jnp.dot(w_t[2 * side * H : 2 * (side + 1) * H, :], normed[:, lanes], preferred_element_type=F32)
            gate, value = jax.nn.sigmoid(pre[:H]), pre[H:]
            product = gate * value
            factors[2 * side * H : (2 * side + 1) * H, lanes] = product * (1.0 - gate)
            factors[(2 * side + 1) * H : 2 * (side + 1) * H, lanes] = gate
            spread(t, product)
        to_planes(planes)

    gated(0, send_first)
    own_op_first = scatter(send_first, firsts.at[y_hi, rows_of(row), :], OP_FIRST)
    gated(1, send_second)

    def pass_on(at, k, to):
        send(cots.at[at, k], cots.at[at, k], RING, (row, to), ring_sem.at[at, k])

    def arrived(at, k):
        wait(cots.at[at, k], ring_sem.at[at, k])

    own_cot.wait()
    wait(send_cot.at[: BAND - 1], recv_sem.at[COT])
    pass_on(x, 0, right)
    pass_on(x, 1, left)
    pass_on(x, 1, right)
    pass_on(x, 0, left)
    own_op_second = scatter(send_second, seconds.at[y_hi, rows_of(row), :], OP_SECOND)
    arrived(left_x, 0)
    pass_on(left_x, 0, right)
    arrived(right_x, 1)
    pass_on(right_x, 1, left)

    own_op_first.wait()
    wait(send_first.at[: BAND - 1], recv_sem.at[OP_FIRST])

    def second_products(at):
        cot = jnp.concatenate([cots[at, 0], cots[at, 1]], 1)
        both = tn(cot, jnp.concatenate([firsts[0], firsts[1]], 1))
        for there in range(YS):
            lanes = slice(there * 2 * W, (there + 1) * 2 * W)
            for k in range(YS):
                out_second[there, pl.ds(pl.multiple_of((YS * at + k) * W, W), W), :] = jnp.where(
                    left_lanes, both[2 * k * W : (2 * k + 1) * W, lanes], both[(2 * k + 1) * W : 2 * (k + 1) * W, lanes]
                ).astype(BF16)

        @pl.loop(0, ROWS // XS)
        def _(d):
            p = at * (ROWS // XS) + d
            mate = 1 - y_hi
            send(out_second.at[mate, rows_of(p), :], got_second.at[plane], SECOND, (p, x * YS + mate))

            @pl.when(p != row)
            def _():
                send(out_second.at[y_hi, rows_of(p), :], got_second.at[plane], SECOND, (p, col))

            @pl.when(p == row)
            def _():
                copy = pltpu.make_async_copy(
                    out_second.at[y_hi, rows_of(p), :], got_second.at[plane], local_sem.at[SECOND]
                )
                copy.start()
                copy.wait()

    second_products(x)
    arrived(right_x, 0)
    second_products(right_x)
    arrived(left_x, 1)
    second_products(left_x)
    arrived(far_x, 0)
    arrived(far_x, 1)
    second_products(far_x)

    own_op_second.wait()
    wait(send_second.at[: BAND - 1], recv_sem.at[OP_SECOND])
    for q in range(COLS):
        for there in range(YS):
            block = seconds[there, q * W : (q + 1) * W, :].astype(F32)
            lanes = slice(there * 2 * W, (there + 1) * 2 * W)
            blocks[q * 2 * W : q * 2 * W + W, lanes] = jnp.where(left_lanes, block, 0.0).astype(BF16)
            blocks[q * 2 * W + W : (q + 1) * 2 * W, lanes] = jnp.where(left_lanes, 0.0, block).astype(BF16)
    for half in range(2):
        rows = slice(half * N // 2, (half + 1) * N // 2)
        cot = jnp.concatenate([cots[q // YS, q % YS, rows] for q in range(COLS)], 1)
        term = jnp.dot(cot, blocks[...], preferred_element_type=F32)
        for there in range(YS):
            out_first[there, rows, :] = term[:, there * 2 * W : (there + 1) * 2 * W].astype(BF16)

    def return_first(there, p):
        send(out_first.at[there, rows_of(p), :], got_first.at[plane], FIRST, (p, x * YS + there))

    each_of_band(return_first)
    own_first = pltpu.make_async_copy(out_first.at[y_hi, rows_of(row), :], got_first.at[plane], local_sem.at[FIRST])
    own_first.start()

    def gather_in(side, got):
        @pl.loop(0, BAND, unroll=8)
        def _(h):
            stage[pl.ds(pl.multiple_of(h * R, R), R), :] = got[h].astype(F32)

        for t in range(R // 2):
            lanes = slice(t * 2 * W, (t + 1) * 2 * W)
            even = stage[pl.ds(2 * t, BAND, stride=R), :]
            odd = stage[pl.ds(2 * t + 1, BAND, stride=R), :]
            grad = jnp.concatenate(
                [
                    jnp.where(left_lanes, even, pltpu.roll(odd, W, 1)),
                    jnp.where(left_lanes, pltpu.roll(even, W, 1), odd),
                ],
                0,
            )
            for m in (2 * side, 2 * side + 1):
                grads[m * H : (m + 1) * H, lanes] = (grad * factors[m * H : (m + 1) * H, lanes]).astype(BF16)

    spot = (y_lo * 2 + core) * COLS + col

    def each_spot(act):
        @pl.loop(1, SPOTS)
        def _(d):
            g = lax.rem(spot + d, SPOTS)
            act(g, (plane_row(g // COLS), lax.rem(g, COLS)))

    def weight_part(side, kind):
        part = nt(normed[...], grads[2 * side * H : 2 * (side + 1) * H, :])
        for m in range(2):
            w_part[(2 * side + m) * H : (2 * side + m + 1) * H, :] = part[:, m * H : (m + 1) * H]

        def share(g):
            return pl.ds(pl.multiple_of(2 * side * H + g * PART, PART), PART)

        mine = slice(side * PART, (side + 1) * PART)
        each_spot(lambda g, device: send(w_part.at[share(g), :], parts.at[spot, mine, :], kind, device))
        parts[spot, mine, :] = w_part[share(spot), :]

    wait(send_cot.at[: BAND - 1], recv_sem.at[SECOND])
    gather_in(1, got_second)
    weight_part(1, PART_SECOND)
    own_first.wait()
    wait(send_cot.at[: BAND - 1], recv_sem.at[FIRST])
    gather_in(0, got_first)
    weight_part(0, PART_FIRST)

    gain_sum = jnp.zeros((H, 2 * W), F32)
    bias_sum = jnp.zeros((H, 2 * W), F32)
    for t in range(R // 2):
        lanes = slice(t * 2 * W, (t + 1) * 2 * W)
        grad = jnp.dot(w_cat[...], grads[:, lanes], preferred_element_type=F32)
        normed_grad[:, lanes] = grad
        gain_sum += grad * scaled[:, lanes]
        bias_sum += grad
    gain_sum = jnp.sum(jnp.transpose(gain_sum), 0, keepdims=True)
    bias_sum = jnp.sum(jnp.transpose(bias_sum), 0, keepdims=True)
    small_z[z] = jnp.concatenate([gain_sum, bias_sum, jnp.zeros((6, H), F32)], 0)

    def z_peer(d):
        return (y_lo * 2 * DEPTH + lax.rem(z + d, DEPTH) * 2 + core, col)

    @pl.loop(1, DEPTH)
    def _(d):
        send(small_z.at[z], small_z.at[z], SMALL_Z, z_peer(d))

    wait(parts.at[: SPOTS - 1, :PART, :], recv_sem.at[PART_SECOND])
    wait(parts.at[: SPOTS - 1, :PART, :], recv_sem.at[PART_FIRST])
    deeps[z] = jnp.sum(parts[...], 0)

    @pl.loop(1, DEPTH)
    def _(d):
        send(deeps.at[z], deeps.at[z], DEEP, z_peer(d))

    for t in range(R // 2):
        lanes = slice(t * 2 * W, (t + 1) * 2 * W)
        scale = scaled[:, lanes]
        grad = normed_grad[:, lanes] * gain
        pair = inverse[t : t + 1, :] * (
            grad - jnp.mean(grad, 0, keepdims=True) - scale * jnp.mean(grad * scale, 0, keepdims=True)
        )
        out_ref[lanes, :] = jnp.transpose(pair).astype(BF16)

    wait(small_z.at[: DEPTH - 1], recv_sem.at[SMALL_Z])
    small_col[col] = jnp.sum(small_z[...], 0)

    @pl.loop(1, COLS)
    def _(d):
        send(small_col.at[col], small_col.at[col], SMALL_COL, (row, lax.rem(col + d, COLS)))

    wait(deeps.at[: DEPTH - 1], recv_sem.at[DEEP])
    wholes[spot] = jnp.sum(deeps[...], 0) * (1.0 / N)
    each_spot(lambda g, device: send(wholes.at[spot], wholes.at[spot], WHOLE, device))

    wait(small_col.at[: COLS - 1], recv_sem.at[SMALL_COL])
    quarter = y_lo * 2 + core
    small_row[quarter] = jnp.sum(small_col[...], 0)

    @pl.loop(1, 4)
    def _(d):
        send(small_row.at[quarter], small_row.at[quarter], SMALL_ROW, (plane_row(lax.rem(quarter + d, 4)), col))

    for kind in (COT, OP_FIRST, OP_SECOND, FIRST, SECOND):
        wait(send_cot.at[: BAND - 1], send_sem.at[kind])
    wait(cots.at[: XS - 1], send_sem.at[RING])
    wait(parts.at[: SPOTS - 1, :PART, :], send_sem.at[PART_SECOND])
    wait(parts.at[: SPOTS - 1, :PART, :], send_sem.at[PART_FIRST])
    wait(deeps.at[: DEPTH - 1], send_sem.at[DEEP])
    wait(small_z.at[: DEPTH - 1], send_sem.at[SMALL_Z])
    wait(small_col.at[: COLS - 1], send_sem.at[SMALL_COL])

    wait(wholes.at[: SPOTS - 1], recv_sem.at[WHOLE])
    for side in range(2):
        wg_ref[2 * side * H : 2 * (side + 1) * H, :] = wholes[:, side * PART : (side + 1) * PART, :].reshape(2 * H, H)
    wait(small_row.at[:3], recv_sem.at[SMALL_ROW])
    total = jnp.sum(small_row[...], 0) * (1.0 / N)
    gg_ref[...] = total[0:1]
    bg_ref[...] = total[1:2]
    wait(wholes.at[: SPOTS - 1], send_sem.at[WHOLE])
    wait(small_row.at[:3], send_sem.at[SMALL_ROW])


def deliver(a, b, c, d, out_a, out_b, out_c, out_d):
    out_a[...] = a[...]
    out_b[...] = b[...]
    out_c[...] = c[...]
    out_d[...] = d[...]


def local(pair_input, norm_gain, norm_bias, weights, cotangent):
    vmem = pl.BlockSpec(memory_space=pltpu.VMEM)
    results = (
        jax.ShapeDtypeStruct((PAIRS, H), BF16),
        jax.ShapeDtypeStruct((4 * H, H), F32),
        jax.ShapeDtypeStruct((1, H), F32),
        jax.ShapeDtypeStruct((1, H), F32),
    )
    computed = pl.pallas_call(
        kernel,
        out_shape=results,
        in_specs=[pl.BlockSpec(memory_space=pltpu.HBM)] * 5,
        out_specs=(vmem,) * 4,
        scratch_shapes=[
            pltpu.VMEM((PAIRS, H), BF16),
            pltpu.VMEM((1, H), F32),
            pltpu.VMEM((1, H), F32),
            pltpu.VMEM((4, H, H), BF16),
            pltpu.VMEM((PAIRS, H), BF16),
            pltpu.VMEM((PAIRS, 2 * W), F32),
            pltpu.VMEM((BAND, R, 2 * W), BF16),
            pltpu.VMEM((BAND, R, 2 * W), BF16),
            pltpu.VMEM((BAND, R, 2 * W), BF16),
            pltpu.VMEM((XS, YS, N, 2 * W), BF16),
            pltpu.VMEM((YS, N, 2 * W), BF16),
            pltpu.VMEM((YS, N, 2 * W), BF16),
            pltpu.VMEM((2 * N, YS * 2 * W), BF16),
            pltpu.VMEM((YS, N, 2 * W), BF16),
            pltpu.VMEM((YS, N, 2 * W), BF16),
            pltpu.VMEM((BAND, R, 2 * W), BF16),
            pltpu.VMEM((BAND, R, 2 * W), BF16),
            pltpu.VMEM((4 * H, PAIRS), F32),
            pltpu.VMEM((H, PAIRS), F32),
            pltpu.VMEM((H, PAIRS), BF16),
            pltpu.VMEM((R // 2, 2 * W), F32),
            pltpu.VMEM((4 * H, H), BF16),
            pltpu.VMEM((H, 4 * H), BF16),
            pltpu.VMEM((4 * H, PAIRS), BF16),
            pltpu.VMEM((H, PAIRS), F32),
            pltpu.VMEM((4 * H, H), F32),
            pltpu.VMEM((SPOTS, 2 * PART, H), F32),
            pltpu.VMEM((DEPTH, 2 * PART, H), F32),
            pltpu.VMEM((SPOTS, 2 * PART, H), F32),
            pltpu.VMEM((DEPTH, 8, H), F32),
            pltpu.VMEM((COLS, 8, H), F32),
            pltpu.VMEM((4, 8, H), F32),
            pltpu.SemaphoreType.DMA((13,)),
            pltpu.SemaphoreType.DMA((13,)),
            pltpu.SemaphoreType.DMA((XS, YS)),
            pltpu.SemaphoreType.DMA((5,)),
            pltpu.SemaphoreType.DMA((5,)),
        ],
        compiler_params=pltpu.CompilerParams(
            collective_id=0, has_side_effects=True, vmem_limit_bytes=60 * 1024 * 1024
        ),
        name="triangle_backward",
    )(
        pair_input.reshape(PAIRS, H),
        norm_gain.reshape(1, H),
        norm_bias.reshape(1, H),
        weights,
        cotangent.reshape(PAIRS, H),
    )
    out, weight_grad, gain_grad, bias_grad = pl.pallas_call(
        deliver,
        out_shape=results,
        in_specs=[vmem] * 4,
        out_specs=(vmem,) * 4,
        name="deliver",
    )(*computed)
    return (
        out.reshape(R, W, H),
        weight_grad.reshape(4, H, H),
        gain_grad.reshape(H),
        bias_grad.reshape(H),
    )


def solution(mesh):
    placed = (P("row", "col", None), P(), P(), P(), P("row", "col", None))
    return jax.shard_map(
        local,
        mesh=mesh,
        in_specs=placed,
        out_specs=(P("row", "col", None), P(), P(), P()),
        check_vma=False,
    )
```

time: 80 us -> 63.5 us (0.79)
  Pallas kernels: 73.2 us -> 62.7 us
  local copies, waits for them, and re-layouts: 5.89 us -> 0 us
    pallas_call x1 -> x2, Pallas kernels: 73.2 us -> 62.7 us  [the longest x1 60.9 us: local(): pl.pallas_call(kernel, out_shape=results, in_specs=[pl.BlockSpec(memory_s...]
    unnamed x14 -> x0, local copies, waits for them, and re-layouts: 5.89 us -> none
where the time goes in v2:
time: 63.5 us; the launch traced here: 63.3 us
  Pallas kernels  62.7 us (99%)
  between operations  0.64 us (1%)
    pallas_call x1, Pallas kernels, local(): pl.pallas_call(kernel, out_shape=results, in_specs=[pl.BlockSpec(memory_s...  60.9 us
    pallas_call x1, Pallas kernels, local(): pl.pallas_call(deliver, out_shape=results, in_specs=[vmem] * 4, out_specs...  1.85 us

profile of v2, /device:TPU:1, one launch (start us, length us, event | category | flops | bytes accessed | tf_op | source)
XLA Modules:
  0.0 63.3 jit_solution(5390682033441564829)
XLA Ops:
  0.6 60.9 %triangle_backward.1 = (bf16[1024,128]{1,0:T(8,128)(2,1)}, f32[512,128]{1,0:T(8,128)}, f32[1,128]{1,0:T(1,128)}, f32[1,128]{1,0:T(1,128)}) custom-call(bf16[1024,128]{1,0:T(8,128)(2,1)} %bitcast.8, f32[1,128]{1,0:T(1,128)} %bitcast.10, f32[1,128]{1,0:T(1,128)} %bitcast.11, bf16[4,128,128]{2,1,0:T(8,128)(2,1)} %w_hbm.1, bf16[1024,128]{1,0:T(8,128)(2,1)} %bitcast.9), custom_call_target="tpu_custom_call" | custom-call | tf_op jit(solution)/shard_map/triangle_backward/pallas_call | solution.py:380
  61.5 1.8 %deliver.1 = (bf16[1024,128]{1,0:T(8,128)(2,1)}, f32[512,128]{1,0:T(8,128)}, f32[1,128]{1,0:T(1,128)}, f32[1,128]{1,0:T(1,128)}) custom-call(bf16[1024,128]{1,0:T(8,128)(2,1)} %get-tuple-element.12.a, f32[512,128]{1,0:T(8,128)} %get-tuple-element.13.b, f32[1,128]{1,0:T(1,128)} %get-tuple-element.14.c, f32[1,128]{1,0:T(1,128)} %get-tuple-element.15.d), custom_call_target="tpu_custom_call" | custom-call | tf_op jit(solution)/shard_map/deliver/pallas_call | solution.py:435

commit v3 on v2

--- a/solution.py
+++ b/solution.py
@@ -16,7 +16,8 @@
 SPOTS = COLS * 4
 PART = 4 * H // SPOTS // 2
 
-COT, OP_FIRST, OP_SECOND, FIRST, SECOND, PART_FIRST, PART_SECOND, DEEP, WHOLE, SMALL_Z, SMALL_COL, SMALL_ROW, RING = range(13)
+COT, OP_FIRST, OP_SECOND, FIRST, SECOND, SMALL_Z, SMALL_COL, SMALL_ROW, RING = range(9)
+PARTS, DEEPS, WHOLES = (9, 10), (11, 12), (13, 14)
 
 
 def nt(a, b):
@@ -33,7 +34,7 @@
     pair_ref, gain_ref, bias_ref, w_ref, cot_ref,
     stage, send_cot, send_first, send_second, cots, firsts, seconds, blocks, out_first, out_second, got_first, got_second,
     factors, scaled, normed, inverse, w_t, w_cat, grads, normed_grad, w_part, parts, deeps, wholes, small_z, small_col, small_row,
-    send_sem, recv_sem, ring_sem, local_sem, load_sem,
+    send_sem, recv_sem, cot_sem, ring_sem, local_sem, load_sem,
 ):
     row, col = lax.axis_index("row"), lax.axis_index("col")
     z, core, y_lo = lax.rem(row // 2, DEPTH), lax.rem(row, 2), row // (2 * DEPTH)
@@ -78,17 +79,19 @@
     for dy in (2, 1, 3, 0):
         other_y = lax.rem(y + dy, 4)
         for dc in (1, 0):
-            near.append((other_y // 2, lax.rem(other_y, 2) * (2 * DEPTH) + lax.rem(core + dc, 2)))
-
-    def each_of_band(act):
+            near.append((other_y // 2, lax.rem(other_y, 2), lax.rem(core + dc, 2)))
+
+    def each_of_band(act, group=near):
+        offsets = [(there, low * (2 * DEPTH) + c) for there, low, c in group]
+
         @pl.loop(0, DEPTH - 1)
         def _(s):
             dz = DEPTH // 2 + ((s + 1) // 2) * (1 - 2 * lax.rem(s, 2))
             base = lax.rem(z + dz, DEPTH) * 2
-            for there, offset in near:
+            for there, offset in offsets:
                 act(there, base + offset)
 
-        for there, offset in near[:-1]:
+        for there, offset in offsets[:-1] if group[-1] is near[-1] else offsets:
             act(there, z * 2 + offset)
 
     barrier = pltpu.get_barrier_semaphore()
@@ -126,7 +129,16 @@
         spread(t, nt(eye, cot_ref[t * 2 * W : (t + 1) * 2 * W, :]))
     to_planes(send_cot)
     pl.semaphore_wait(barrier, BAND - 1 + 2)
-    own_cot = scatter(send_cot, cots.at[x, y_hi, rows_of(row), :], COT)
+
+    def send_cot_to(there, p):
+        send(
+            send_cot.at[there * ROWS + p], cots.at[x, y_hi, rows_of(row), :], COT, (p, x * YS + there), cot_sem.at[y]
+        )
+
+    for dy in (3, 1, 2, 0):
+        each_of_band(send_cot_to, near[2 * dy : 2 * dy + 2])
+    own_cot = pltpu.make_async_copy(send_cot.at[plane], cots.at[x, y_hi, rows_of(row), :], local_sem.at[COT])
+    own_cot.start()
 
     for load in loads[1:]:
         load.wait()
@@ -156,31 +168,40 @@
             spread(t, product)
         to_planes(planes)
 
+    pieces = [lax.rem(y + dy, 4) for dy in (0, 3, 1, 2)]
+
+    def pass_on(at, g, to):
+        piece = cots.at[at, g // 2, pl.ds(pl.multiple_of(lax.rem(g, 2) * (N // 2), N // 2), N // 2), :]
+        send(piece, piece, RING, (row, to), ring_sem.at[at, g])
+
+    def arrived(at, g):
+        wait(cots.at[0, 0, : N // 2, :], ring_sem.at[at, g])
+
+    def start_round(i):
+        wait(send_cot.at[: BAND // 4 - (i == 0)], cot_sem.at[pieces[i]])
+        pass_on(x, pieces[i], right)
+        pass_on(x, pieces[i], left)
+
     gated(0, send_first)
     own_op_first = scatter(send_first, firsts.at[y_hi, rows_of(row), :], OP_FIRST)
+    own_cot.wait()
+    start_round(0)
     gated(1, send_second)
-
-    def pass_on(at, k, to):
-        send(cots.at[at, k], cots.at[at, k], RING, (row, to), ring_sem.at[at, k])
-
-    def arrived(at, k):
-        wait(cots.at[at, k], ring_sem.at[at, k])
-
-    own_cot.wait()
-    wait(send_cot.at[: BAND - 1], recv_sem.at[COT])
-    pass_on(x, 0, right)
-    pass_on(x, 1, left)
-    pass_on(x, 1, right)
-    pass_on(x, 0, left)
     own_op_second = scatter(send_second, seconds.at[y_hi, rows_of(row), :], OP_SECOND)
-    arrived(left_x, 0)
-    pass_on(left_x, 0, right)
-    arrived(right_x, 1)
-    pass_on(right_x, 1, left)
+    start_round(1)
+    start_round(2)
+    arrived(left_x, pieces[0])
+    pass_on(left_x, pieces[0], right)
+    start_round(3)
+    arrived(right_x, pieces[1])
+    pass_on(right_x, pieces[1], left)
+    arrived(left_x, pieces[2])
+    pass_on(left_x, pieces[2], right)
+    arrived(right_x, pieces[3])
+    pass_on(right_x, pieces[3], left)
 
     own_op_first.wait()
     wait(send_first.at[: BAND - 1], recv_sem.at[OP_FIRST])
-
     def second_products(at):
         cot = jnp.concatenate([cots[at, 0], cots[at, 1]], 1)
         both = tn(cot, jnp.concatenate([firsts[0], firsts[1]], 1))
@@ -210,12 +231,14 @@
                 copy.wait()
 
     second_products(x)
-    arrived(right_x, 0)
+    arrived(left_x, pieces[1])
+    arrived(left_x, pieces[3])
+    second_products(left_x)
+    arrived(right_x, pieces[0])
+    arrived(right_x, pieces[2])
     second_products(right_x)
-    arrived(left_x, 1)
-    second_products(left_x)
-    arrived(far_x, 0)
-    arrived(far_x, 1)
+    for i in range(4):
+        arrived(far_x, pieces[i])
     second_products(far_x)
 
     own_op_second.wait()
@@ -262,12 +285,23 @@
     spot = (y_lo * 2 + core) * COLS + col
 
     def each_spot(act):
-        @pl.loop(1, SPOTS)
-        def _(d):
-            g = lax.rem(spot + d, SPOTS)
-            act(g, (plane_row(g // COLS), lax.rem(g, COLS)))
-
-    def weight_part(side, kind):
+        beside = [((low * 2 + c) * COLS + there, low * (2 * DEPTH) + z * 2 + c, there) for there, low, c in near]
+
+        def visit(there_x, spots):
+            for g, p, there in spots:
+                act(g + there_x * YS, (p, there_x * YS + there))
+
+        for dx in (2, 1, 3):
+            visit(lax.rem(x + dx, XS), beside)
+        visit(x, beside[:-1])
+
+    def z_peer(d):
+        return (y_lo * 2 * DEPTH + lax.rem(z + d, DEPTH) * 2 + core, col)
+
+    def mine(side):
+        return slice(side * PART, (side + 1) * PART)
+
+    def weight_part(side):
         part = nt(normed[...], grads[2 * side * H : 2 * (side + 1) * H, :])
         for m in range(2):
             w_part[(2 * side + m) * H : (2 * side + m + 1) * H, :] = part[:, m * H : (m + 1) * H]
@@ -275,17 +309,32 @@
         def share(g):
             return pl.ds(pl.multiple_of(2 * side * H + g * PART, PART), PART)
 
-        mine = slice(side * PART, (side + 1) * PART)
-        each_spot(lambda g, device: send(w_part.at[share(g), :], parts.at[spot, mine, :], kind, device))
-        parts[spot, mine, :] = w_part[share(spot), :]
+        each_spot(lambda g, device: send(w_part.at[share(g), :], parts.at[spot, mine(side), :], PARTS[side], device))
+        parts[spot, mine(side), :] = w_part[share(spot), :]
+
+    def weight_deep(side):
+        wait(parts.at[: SPOTS - 1, :PART, :], recv_sem.at[PARTS[side]])
+        deeps[z, mine(side), :] = jnp.sum(parts[:, mine(side), :], 0)
+        own = deeps.at[z, mine(side), :]
+
+        @pl.loop(1, DEPTH)
+        def _(d):
+            send(own, own, DEEPS[side], z_peer(d))
+
+    def weight_whole(side):
+        wait(deeps.at[: DEPTH - 1, :PART, :], recv_sem.at[DEEPS[side]])
+        wholes[spot, mine(side), :] = jnp.sum(deeps[:, mine(side), :], 0) * (1.0 / N)
+        own = wholes.at[spot, mine(side), :]
+        each_spot(lambda g, device: send(own, own, WHOLES[side], device))
 
     wait(send_cot.at[: BAND - 1], recv_sem.at[SECOND])
     gather_in(1, got_second)
-    weight_part(1, PART_SECOND)
+    weight_part(1)
     own_first.wait()
     wait(send_cot.at[: BAND - 1], recv_sem.at[FIRST])
     gather_in(0, got_first)
-    weight_part(0, PART_FIRST)
+    weight_part(0)
+    weight_deep(1)
 
     gain_sum = jnp.zeros((H, 2 * W), F32)
     bias_sum = jnp.zeros((H, 2 * W), F32)
@@ -299,20 +348,12 @@
     bias_sum = jnp.sum(jnp.transpose(bias_sum), 0, keepdims=True)
     small_z[z] = jnp.concatenate([gain_sum, bias_sum, jnp.zeros((6, H), F32)], 0)
 
-    def z_peer(d):
-        return (y_lo * 2 * DEPTH + lax.rem(z + d, DEPTH) * 2 + core, col)
-
     @pl.loop(1, DEPTH)
     def _(d):
         send(small_z.at[z], small_z.at[z], SMALL_Z, z_peer(d))
 
-    wait(parts.at[: SPOTS - 1, :PART, :], recv_sem.at[PART_SECOND])
-    wait(parts.at[: SPOTS - 1, :PART, :], recv_sem.at[PART_FIRST])
-    deeps[z] = jnp.sum(parts[...], 0)
-
-    @pl.loop(1, DEPTH)
-    def _(d):
-        send(deeps.at[z], deeps.at[z], DEEP, z_peer(d))
+    weight_deep(0)
+    weight_whole(1)
 
     for t in range(R // 2):
         lanes = slice(t * 2 * W, (t + 1) * 2 * W)
@@ -330,9 +371,7 @@
     def _(d):
         send(small_col.at[col], small_col.at[col], SMALL_COL, (row, lax.rem(col + d, COLS)))
 
-    wait(deeps.at[: DEPTH - 1], recv_sem.at[DEEP])
-    wholes[spot] = jnp.sum(deeps[...], 0) * (1.0 / N)
-    each_spot(lambda g, device: send(wholes.at[spot], wholes.at[spot], WHOLE, device))
+    weight_whole(0)
 
     wait(small_col.at[: COLS - 1], recv_sem.at[SMALL_COL])
     quarter = y_lo * 2 + core
@@ -345,20 +384,20 @@
     for kind in (COT, OP_FIRST, OP_SECOND, FIRST, SECOND):
         wait(send_cot.at[: BAND - 1], send_sem.at[kind])
     wait(cots.at[: XS - 1], send_sem.at[RING])
-    wait(parts.at[: SPOTS - 1, :PART, :], send_sem.at[PART_SECOND])
-    wait(parts.at[: SPOTS - 1, :PART, :], send_sem.at[PART_FIRST])
-    wait(deeps.at[: DEPTH - 1], send_sem.at[DEEP])
+    for side in range(2):
+        wait(parts.at[: SPOTS - 1, :PART, :], send_sem.at[PARTS[side]])
+        wait(deeps.at[: DEPTH - 1, :PART, :], send_sem.at[DEEPS[side]])
     wait(small_z.at[: DEPTH - 1], send_sem.at[SMALL_Z])
     wait(small_col.at[: COLS - 1], send_sem.at[SMALL_COL])
 
-    wait(wholes.at[: SPOTS - 1], recv_sem.at[WHOLE])
-    for side in range(2):
-        wg_ref[2 * side * H : 2 * (side + 1) * H, :] = wholes[:, side * PART : (side + 1) * PART, :].reshape(2 * H, H)
     wait(small_row.at[:3], recv_sem.at[SMALL_ROW])
     total = jnp.sum(small_row[...], 0) * (1.0 / N)
     gg_ref[...] = total[0:1]
     bg_ref[...] = total[1:2]
-    wait(wholes.at[: SPOTS - 1], send_sem.at[WHOLE])
+    for side in (1, 0):
+        wait(wholes.at[: SPOTS - 1, :PART, :], recv_sem.at[WHOLES[side]])
+        wg_ref[2 * side * H : 2 * (side + 1) * H, :] = wholes[:, mine(side), :].reshape(2 * H, H)
+        wait(wholes.at[: SPOTS - 1, :PART, :], send_sem.at[WHOLES[side]])
     wait(small_row.at[:3], send_sem.at[SMALL_ROW])
 
 
@@ -415,28 +454,35 @@
             pltpu.VMEM((DEPTH, 8, H), F32),
             pltpu.VMEM((COLS, 8, H), F32),
             pltpu.VMEM((4, 8, H), F32),
-            pltpu.SemaphoreType.DMA((13,)),
-            pltpu.SemaphoreType.DMA((13,)),
-            pltpu.SemaphoreType.DMA((XS, YS)),
+            pltpu.SemaphoreType.DMA((15,)),
+            pltpu.SemaphoreType.DMA((15,)),
+            pltpu.SemaphoreType.DMA((4,)),
+            pltpu.SemaphoreType.DMA((XS, 4)),
             pltpu.SemaphoreType.DMA((5,)),
             pltpu.SemaphoreType.DMA((5,)),
         ],
         compiler_params=pltpu.CompilerParams(
-            collective_id=0, has_side_effects=True, vmem_limit_bytes=60 * 1024 * 1024
+            collective_id=0, has_side_effects=True, vmem_limit_bytes=40 * 1024 * 1024
         ),
         name="triangle_backward",
     )(
-        pair_input.reshape(PAIRS, H),
-        norm_gain.reshape(1, H),
-        norm_bias.reshape(1, H),
-        weights,
-        cotangent.reshape(PAIRS, H),
+        *(
+            pltpu.with_memory_space_constraint(a, pltpu.HBM)
+            for a in (
+                pair_input.reshape(PAIRS, H),
+                norm_gain.reshape(1, H),
+                norm_bias.reshape(1, H),
+                weights,
+                cotangent.reshape(PAIRS, H),
+            )
+        ),
     )
     out, weight_grad, gain_grad, bias_grad = pl.pallas_call(
         deliver,
         out_shape=results,
         in_specs=[vmem] * 4,
         out_specs=(vmem,) * 4,
+        compiler_params=pltpu.CompilerParams(vmem_limit_bytes=4 * 1024 * 1024),
         name="deliver",
     )(*computed)
     return (

time: 63.5 us -> 60.1 us (0.946)
  Pallas kernels: 62.7 us -> 59.4 us
    pallas_call x1, Pallas kernels: 60.9 us -> 58.6 us  [local(): pl.pallas_call(kernel, out_shape=results, in_specs=[pl.BlockSpec(memory_s...]
    pallas_call x1, Pallas kernels: 1.85 us -> 0.83 us  [local(): pl.pallas_call(deliver, out_shape=results, in_specs=[vmem] * 4, out_specs...]
where the time goes in v3:
time: 60.1 us; the launch traced here: 60 us
  Pallas kernels  59.4 us (99%)
  between operations  0.64 us (1%)
    pallas_call x1, Pallas kernels, local(): pl.pallas_call(kernel, out_shape=results, in_specs=[pl.BlockSpec(memory_s...  58.6 us

profile of v3, /device:TPU:1, one launch (start us, length us, event | category | flops | bytes accessed | tf_op | source)
XLA Modules:
  0.0 60.0 jit_solution(4272103783400144349)
XLA Ops:
  0.6 58.6 %triangle_backward.1 = (bf16[1024,128]{1,0:T(8,128)(2,1)S(1)}, f32[512,128]{1,0:T(8,128)S(1)}, f32[1,128]{1,0:T(1,128)S(1)}, f32[1,128]{1,0:T(1,128)S(1)}) custom-call(bf16[1024,128]{1,0:T(8,128)(2,1)} %bitcast.8, f32[1,128]{1,0:T(1,128)} %bitcast.10, f32[1,128]{1,0:T(1,128)} %bitcast.11, bf16[4,128,128]{2,1,0:T(8,128)(2,1)} %w_hbm.1, bf16[1024,128]{1,0:T(8,128)(2,1)} %bitcast.9), custom_call_target="tpu_custom_call" | custom-call | tf_op jit(solution)/shard_map/triangle_backward/pallas_call | solution.py:419
  59.2 0.8 %deliver.1 = (bf16[1024,128]{1,0:T(8,128)(2,1)}, f32[512,128]{1,0:T(8,128)}, f32[1,128]{1,0:T(1,128)}, f32[1,128]{1,0:T(1,128)}) custom-call(bf16[1024,128]{1,0:T(8,128)(2,1)S(1)} %get-tuple-element.12.a, f32[512,128]{1,0:T(8,128)S(1)} %get-tuple-element.13.b, f32[1,128]{1,0:T(1,128)S(1)} %get-tuple-element.14.c, f32[1,128]{1,0:T(1,128)S(1)} %get-tuple-element.15.d), custom_call_target="tpu_custom_call" | custom-call | tf_op jit(solution)/shard_map/deliver/pallas_call | solution.py:480

commit v4 on v3

--- a/solution.py
+++ b/solution.py
@@ -34,7 +34,7 @@
     pair_ref, gain_ref, bias_ref, w_ref, cot_ref,
     stage, send_cot, send_first, send_second, cots, firsts, seconds, blocks, out_first, out_second, got_first, got_second,
     factors, scaled, normed, inverse, w_t, w_cat, grads, normed_grad, w_part, parts, deeps, wholes, small_z, small_col, small_row,
-    send_sem, recv_sem, cot_sem, ring_sem, local_sem, load_sem,
+    send_sem, recv_sem, cot_sem, ring_sem, local_sem, load_sem, ready_sem,
 ):
     row, col = lax.axis_index("row"), lax.axis_index("col")
     z, core, y_lo = lax.rem(row // 2, DEPTH), lax.rem(row, 2), row // (2 * DEPTH)
@@ -101,7 +101,10 @@
     def greet(there, p):
         pl.semaphore_signal(barrier, inc=1, device_id=(p, x * YS + there), device_id_type=MESH)
 
-    each_of_band(greet)
+    each_of_band(greet, near[6:])
+    others_y = [(near[2 * i + 1][0], near[2 * i + 1][1] * (2 * DEPTH) + z * 2 + core) for i in range(3)]
+    for there, p in others_y:
+        greet(there, p)
     for to in (right, left):
         pl.semaphore_signal(barrier, inc=1, device_id=(row, to), device_id_type=MESH)
 
@@ -115,11 +118,13 @@
         def _(h):
             planes[h] = stage[pl.ds(h, R, stride=BAND), :].astype(BF16)
 
-    def scatter(planes, dst, kind):
+    def scatter(planes, dst, kind, group):
         def act(there, p):
             send(planes.at[there * ROWS + p], dst, kind, (p, x * YS + there))
 
-        each_of_band(act)
+        each_of_band(act, group)
+        if group[-1] is not near[-1]:
+            return None
         own = pltpu.make_async_copy(planes.at[plane], dst, local_sem.at[kind])
         own.start()
         return own
@@ -128,15 +133,16 @@
     for t in range(R // 2):
         spread(t, nt(eye, cot_ref[t * 2 * W : (t + 1) * 2 * W, :]))
     to_planes(send_cot)
-    pl.semaphore_wait(barrier, BAND - 1 + 2)
+    pl.semaphore_wait(barrier, BAND // 4 - 1 + 3 + 2)
+    for there, p in others_y:
+        pl.semaphore_signal(ready_sem, inc=1, device_id=(p, x * YS + there), device_id_type=MESH)
 
     def send_cot_to(there, p):
         send(
             send_cot.at[there * ROWS + p], cots.at[x, y_hi, rows_of(row), :], COT, (p, x * YS + there), cot_sem.at[y]
         )
 
-    for dy in (3, 1, 2, 0):
-        each_of_band(send_cot_to, near[2 * dy : 2 * dy + 2])
+    each_of_band(send_cot_to, near[6:])
     own_cot = pltpu.make_async_copy(send_cot.at[plane], cots.at[x, y_hi, rows_of(row), :], local_sem.at[COT])
     own_cot.start()
 
@@ -183,11 +189,15 @@
         pass_on(x, pieces[i], left)
 
     gated(0, send_first)
-    own_op_first = scatter(send_first, firsts.at[y_hi, rows_of(row), :], OP_FIRST)
+    own_op_first = scatter(send_first, firsts.at[y_hi, rows_of(row), :], OP_FIRST, near[6:])
+    pl.semaphore_wait(ready_sem, 3)
+    for dy in (1, 2, 0):
+        each_of_band(send_cot_to, near[2 * dy : 2 * dy + 2])
+    scatter(send_first, firsts.at[y_hi, rows_of(row), :], OP_FIRST, near[:6])
     own_cot.wait()
     start_round(0)
     gated(1, send_second)
-    own_op_second = scatter(send_second, seconds.at[y_hi, rows_of(row), :], OP_SECOND)
+    own_op_second = scatter(send_second, seconds.at[y_hi, rows_of(row), :], OP_SECOND, near)
     start_round(1)
     start_round(2)
     arrived(left_x, pieces[0])
@@ -460,6 +470,7 @@
             pltpu.SemaphoreType.DMA((XS, 4)),
             pltpu.SemaphoreType.DMA((5,)),
             pltpu.SemaphoreType.DMA((5,)),
+            pltpu.SemaphoreType.REGULAR,
         ],
         compiler_params=pltpu.CompilerParams(
             collective_id=0, has_side_effects=True, vmem_limit_bytes=40 * 1024 * 1024

time: 60.1 us -> 59.4 us (0.988)
  Pallas kernels: 59.4 us -> 58.6 us
    pallas_call x1, Pallas kernels: 58.6 us -> 57.8 us  [local(): pl.pallas_call(kernel, out_shape=results, in_specs=[pl.BlockSpec(memory_s...]
where the time goes in v4:
time: 59.4 us; the launch traced here: 59.3 us
  Pallas kernels  58.6 us (99%)
  between operations  0.64 us (1%)
    pallas_call x1, Pallas kernels, local(): pl.pallas_call(kernel, out_shape=results, in_specs=[pl.BlockSpec(memory_s...  57.8 us

profile of v4, /device:TPU:1, one launch (start us, length us, event | category | flops | bytes accessed | tf_op | source)
XLA Modules:
  0.0 59.3 jit_solution(13752895840070118726)
XLA Ops:
  0.6 57.8 %triangle_backward.1 = (bf16[1024,128]{1,0:T(8,128)(2,1)S(1)}, f32[512,128]{1,0:T(8,128)S(1)}, f32[1,128]{1,0:T(1,128)S(1)}, f32[1,128]{1,0:T(1,128)S(1)}) custom-call(bf16[1024,128]{1,0:T(8,128)(2,1)} %bitcast.8, f32[1,128]{1,0:T(1,128)} %bitcast.10, f32[1,128]{1,0:T(1,128)} %bitcast.11, bf16[4,128,128]{2,1,0:T(8,128)(2,1)} %w_hbm.1, bf16[1024,128]{1,0:T(8,128)(2,1)} %bitcast.9), custom_call_target="tpu_custom_call" | custom-call | tf_op jit(solution)/shard_map/triangle_backward/pallas_call | solution.py:429
  58.5 0.8 %deliver.1 = (bf16[1024,128]{1,0:T(8,128)(2,1)}, f32[512,128]{1,0:T(8,128)}, f32[1,128]{1,0:T(1,128)}, f32[1,128]{1,0:T(1,128)}) custom-call(bf16[1024,128]{1,0:T(8,128)(2,1)S(1)} %get-tuple-element.12.a, f32[512,128]{1,0:T(8,128)S(1)} %get-tuple-element.13.b, f32[1,128]{1,0:T(1,128)S(1)} %get-tuple-element.14.c, f32[1,128]{1,0:T(1,128)S(1)} %get-tuple-element.15.d), custom_call_target="tpu_custom_call" | custom-call | tf_op jit(solution)/shard_map/deliver/pallas_call | solution.py:491

commit v5 on v4

--- a/solution.py
+++ b/solution.py
@@ -193,9 +193,9 @@
     pl.semaphore_wait(ready_sem, 3)
     for dy in (1, 2, 0):
         each_of_band(send_cot_to, near[2 * dy : 2 * dy + 2])
-    scatter(send_first, firsts.at[y_hi, rows_of(row), :], OP_FIRST, near[:6])
     own_cot.wait()
     start_round(0)
+    scatter(send_first, firsts.at[y_hi, rows_of(row), :], OP_FIRST, near[:6])
     gated(1, send_second)
     own_op_second = scatter(send_second, seconds.at[y_hi, rows_of(row), :], OP_SECOND, near)
     start_round(1)

time: 59.4 us -> 59.4 us (level)
  no operation moved by 1% of the time
where the time goes in v5:
time: 59.4 us; the launch traced here: 59.3 us
  Pallas kernels  58.7 us (99%)
  between operations  0.64 us (1%)
    pallas_call x1, Pallas kernels, local(): pl.pallas_call(kernel, out_shape=results, in_specs=[pl.BlockSpec(memory_s...  57.9 us

profile of v5, /device:TPU:1, one launch (start us, length us, event | category | flops | bytes accessed | tf_op | source)
XLA Modules:
  0.0 59.3 jit_solution(16574827066255107722)
XLA Ops:
  0.6 57.9 %triangle_backward.1 = (bf16[1024,128]{1,0:T(8,128)(2,1)S(1)}, f32[512,128]{1,0:T(8,128)S(1)}, f32[1,128]{1,0:T(1,128)S(1)}, f32[1,128]{1,0:T(1,128)S(1)}) custom-call(bf16[1024,128]{1,0:T(8,128)(2,1)} %bitcast.8, f32[1,128]{1,0:T(1,128)} %bitcast.10, f32[1,128]{1,0:T(1,128)} %bitcast.11, bf16[4,128,128]{2,1,0:T(8,128)(2,1)} %w_hbm.1, bf16[1024,128]{1,0:T(8,128)(2,1)} %bitcast.9), custom_call_target="tpu_custom_call" | custom-call | tf_op jit(solution)/shard_map/triangle_backward/pallas_call | solution.py:429
  58.5 0.8 %deliver.1 = (bf16[1024,128]{1,0:T(8,128)(2,1)}, f32[512,128]{1,0:T(8,128)}, f32[1,128]{1,0:T(1,128)}, f32[1,128]{1,0:T(1,128)}) custom-call(bf16[1024,128]{1,0:T(8,128)(2,1)S(1)} %get-tuple-element.12.a, f32[512,128]{1,0:T(8,128)S(1)} %get-tuple-element.13.b, f32[1,128]{1,0:T(1,128)S(1)} %get-tuple-element.14.c, f32[1,128]{1,0:T(1,128)S(1)} %get-tuple-element.15.d), custom_call_target="tpu_custom_call" | custom-call | tf_op jit(solution)/shard_map/deliver/pallas_call | solution.py:491

commit v6 on v4

--- a/solution.py
+++ b/solution.py
@@ -411,11 +411,15 @@
     wait(small_row.at[:3], send_sem.at[SMALL_ROW])
 
 
-def deliver(a, b, c, d, out_a, out_b, out_c, out_d):
-    out_a[...] = a[...]
-    out_b[...] = b[...]
-    out_c[...] = c[...]
-    out_d[...] = d[...]
+def deliver(a, b, c, d, out_a, out_b, out_c, out_d, sem):
+    copies = [
+        pltpu.make_async_copy(src, dst, sem.at[i])
+        for i, (src, dst) in enumerate(((a, out_a), (b, out_b), (c, out_c), (d, out_d)))
+    ]
+    for copy in copies:
+        copy.start()
+    for copy in copies:
+        copy.wait()
 
 
 def local(pair_input, norm_gain, norm_bias, weights, cotangent):
@@ -492,7 +496,8 @@
         deliver,
         out_shape=results,
         in_specs=[vmem] * 4,
-        out_specs=(vmem,) * 4,
+        out_specs=(pl.BlockSpec(memory_space=pltpu.HBM),) * 4,
+        scratch_shapes=[pltpu.SemaphoreType.DMA((4,))],
         compiler_params=pltpu.CompilerParams(vmem_limit_bytes=4 * 1024 * 1024),
         name="deliver",
     )(*computed)

time: 59.4 us -> 59.4 us (level)
  no operation moved by 1% of the time
where the time goes in v6:
time: 59.4 us; the launch traced here: 59.3 us
  Pallas kernels  58.6 us (99%)
  between operations  0.64 us (1%)
    pallas_call x1, Pallas kernels, local(): pl.pallas_call(kernel, out_shape=results, in_specs=[pl.BlockSpec(memory_s...  57.8 us

profile of v6, /device:TPU:1, one launch (start us, length us, event | category | flops | bytes accessed | tf_op | source)
XLA Modules:
  0.0 59.3 jit_solution(10589108594056185661)
XLA Ops:
  0.6 57.8 %triangle_backward.1 = (bf16[1024,128]{1,0:T(8,128)(2,1)S(1)}, f32[512,128]{1,0:T(8,128)S(1)}, f32[1,128]{1,0:T(1,128)S(1)}, f32[1,128]{1,0:T(1,128)S(1)}) custom-call(bf16[1024,128]{1,0:T(8,128)(2,1)} %bitcast.8, f32[1,128]{1,0:T(1,128)} %bitcast.10, f32[1,128]{1,0:T(1,128)} %bitcast.11, bf16[4,128,128]{2,1,0:T(8,128)(2,1)} %w_hbm.1, bf16[1024,128]{1,0:T(8,128)(2,1)} %bitcast.9), custom_call_target="tpu_custom_call" | custom-call | tf_op jit(solution)/shard_map/triangle_backward/pallas_call | solution.py:433
  58.5 0.8 %deliver.1 = (bf16[1024,128]{1,0:T(8,128)(2,1)}, f32[512,128]{1,0:T(8,128)}, f32[1,128]{1,0:T(1,128)}, f32[1,128]{1,0:T(1,128)}) custom-call(bf16[1024,128]{1,0:T(8,128)(2,1)S(1)} %get-tuple-element.12.a, f32[512,128]{1,0:T(8,128)S(1)} %get-tuple-element.13.b, f32[1,128]{1,0:T(1,128)S(1)} %get-tuple-element.14.c, f32[1,128]{1,0:T(1,128)S(1)} %get-tuple-element.15.d), custom_call_target="tpu_custom_call" | custom-call | tf_op jit(solution)/shard_map/deliver/pallas_call | solution.py:495
